TPU v7x, 128 devices: a whole 4x4x4 slice. The times are simulated.
128 devices in a mesh: section: 8 (over z, y_lo), seq: 16 (over y_hi, x, core).
Axes of the slice: x: 4, y: 4 (y_hi: 2, y_lo: 2; y = y_hi * 2 + y_lo), z: 4, core: 2. Of those that a mesh axis runs over, the one named last changes fastest.
Arguments:
- qkv: bfloat16 [8, 1536, 3, 4096], P('section', 'seq'), may hold values from -5 to 5
- cache: bfloat16 [2, 24, 512, 4096], P(None, 'section', None, 'seq'), may hold values from -5 to 5
- window: int32 [8], P('section'), may hold values from 1 to 24, as said below
Outputs:
- attended: bfloat16 [8, 1536, 4096], P('section', 'seq')
- new_cache: bfloat16 [2, 24, 512, 4096], P(None, 'section', None, 'seq')
Inputs may be any that keep to these rules, and one draw needn't show every extreme that they name: `window`: some section attends all 24 cache frames and some section only the newest.
All inputs are finite; a program needn't handle non-finite values.
Results may differ from a plain program's by a relative error of at most 0.02.
Values may be sent and summed in bfloat16 or wider, within the bound.
No kernel may reach another device: no remote copies, remote signals or barrier semaphores. Data moves between devices by JAX's collectives and lax.ppermute only.
A program may use at most 192 MiB of HBM per device.

v0:
```python
import jax
import jax.numpy as jnp
from jax import lax
from jax.sharding import PartitionSpec as P

HD = 128
CF = 3


def passed_along(value, axis, steps):
    count = lax.axis_size(axis)
    leading, last = (max(0, -steps), min(count, count - steps))
    return lax.ppermute(value, axis, [(source, source + steps) for source in range(leading, last)])


def frame_update(state, query, key_block, value_block, valid):
    running, total, accum = state
    scores = jnp.einsum("qhd,khd->qhk", query, key_block, preferred_element_type=jnp.float32)
    scores = scores * query.shape[-1] ** (-0.5)
    masked = jnp.where(valid, scores, -1e30)
    newest = jnp.maximum(running, jnp.max(masked, axis=-1))
    weights = jnp.where(valid, jnp.exp(scores - newest[..., None]), 0.0)
    factor = jnp.exp(running - newest)
    total = total * factor + jnp.sum(weights, axis=-1)
    mixed = jnp.einsum(
        "qhk,khd->qhd",
        weights.astype(jnp.bfloat16),
        value_block,
        preferred_element_type=jnp.float32,
    )
    accum = accum * factor[..., None] + mixed
    return (newest, total, accum)


def per_device(qkv, cache, window):
    denoise_count = lax.axis_size("section")
    tok_rows = qkv.shape[1]
    all_heads = qkv.shape[3] // HD
    local = qkv.reshape(tok_rows, 3, all_heads, HD)
    spread = lax.all_to_all(local, "seq", split_axis=2, concat_axis=0, tiled=True)
    query = spread[:, 0]
    keys = spread[:, 1]
    values = spread[:, 2]
    span_rows = query.shape[0]
    frame = span_rows // CF
    group = query.shape[1]
    query_frame = jnp.arange(span_rows) // frame
    start_state = (
        jnp.full((span_rows, group), -1e30, jnp.float32),
        jnp.zeros((span_rows, group), jnp.float32),
        jnp.zeros((span_rows, group, HD), jnp.float32),
    )
    state = start_state
    for key_frame in range(CF):
        valid = (query_frame >= key_frame)[:, None, None]
        state = frame_update(
            state,
            query,
            keys[key_frame * frame : (key_frame + 1) * frame],
            values[key_frame * frame : (key_frame + 1) * frame],
            valid,
        )
    frames_dev = cache.shape[1]
    cache_frames = frames_dev * denoise_count
    denoise_index = lax.axis_index("section")
    oldest = cache_frames - window[0]
    carry = state
    key_piece = lax.all_gather(cache[0], "section", axis=0, tiled=True)
    value_piece = lax.all_gather(cache[1], "section", axis=0, tiled=True)
    count = key_piece.shape[0]
    key_rows = key_piece.reshape(count, key_piece.shape[1], group, HD)
    value_rows = value_piece.reshape(count, value_piece.shape[1], group, HD)

    def advance(inner, item):
        offset, key_block, value_block = item
        return (frame_update(inner, query, key_block, value_block, offset >= oldest), None)

    carry, _ = lax.scan(advance, carry, (jnp.arange(count, dtype=jnp.int32), key_rows, value_rows))
    state = carry
    running, total, accum = state
    result = (accum / total[..., None]).astype(jnp.bfloat16)
    returned = lax.all_to_all(result, "seq", split_axis=0, concat_axis=1, tiled=True)
    attended = returned.reshape(1, tok_rows, all_heads * HD)
    fresh = jnp.stack([keys, values]).reshape(2, CF, frame, group * HD)
    rolled = passed_along(cache, "section", -1)
    new_cache = jnp.where(denoise_index == denoise_count - 1, fresh, rolled)
    return (attended, new_cache)


def solution(mesh):
    in_specs = (P("section", "seq", None, None), P(None, "section", None, "seq"), P("section"))
    out_specs = (P("section", "seq", None), P(None, "section", None, "seq"))
    return jax.shard_map(
        per_device, mesh=mesh, in_specs=in_specs, out_specs=out_specs, check_vma=False
    )
```

profile of v0, /device:TPU:1, one launch (start us, length us, event | category | flops | bytes accessed | tf_op | source)
XLA Modules:
  0.0 558.6 jit_solution(18189803596885018236)
XLA Ops:
  7.2 2.8 slice_bitcast_fusion.1
  13.7 8.4 %all-to-all-start = ((bf16[96,3,32,128]{3,0,1,2:T(8,128)(2,1)}), bf16[96,3,32,128]{3,0,1,2:T(8,128)(2,1)S(1)}, u32[]{:S(2)}, u32[]{:S(2)}) async-start(bf16[96,3,32,128]{3,0,1,2:T(8,128)(2,1)} %copy.58), calls=%async_computation | async-start | bytes 4718592 | tf_op jit(solution)/shard_map/all_to_all | solution.py:40
  24.1 34.1 %all-to-all-done = bf16[96,3,32,128]{3,0,1,2:T(8,128)(2,1)S(1)} async-done(((bf16[96,3,32,128]{3,0,1,2:T(8,128)(2,1)}), bf16[96,3,32,128]{3,0,1,2:T(8,128)(2,1)S(1)}, u32[]{:S(2)}, u32[]{:S(2)}) %all-to-all-start) | async-done | bytes 2359328 | tf_op jit(solution)/shard_map/all_to_all | solution.py:40
  62.7 2.7 fusion.36
  69.1 3.8 fusion.74
  74.8 2.9 fusion.101
  77.7 124.0 %all-gather.5.cloned.1.call-done = bf16[1,24,512,256]{3,2,0,1:T(8,128)(2,1)} async-done(((bf16[1,3,512,256]{3,2,0,1:T(8,128)(2,1)}), bf16[1,24,512,256]{3,2,0,1:T(8,128)(2,1)}) %all-gather.5.cloned.1.call-update) | async-done | bytes 6291472 | tf_op jit(solution)/shard_map/all_gather | solution.py:68
  201.7 8.7 %copy.65 = bf16[1,24,512,256]{2,3,1,0:T(8,128)(2,1)} copy(bf16[1,24,512,256]{3,2,0,1:T(8,128)(2,1)} %all-gather.5.cloned.1.call-done) | data formatting | bytes 12582912 | tf_op jit(solution)/shard_map/all_gather | solution.py:68
  210.4 123.7 %all-gather.7.cloned.1.call-done = bf16[1,24,512,256]{3,2,0,1:T(8,128)(2,1)} async-done(((bf16[1,3,512,256]{3,2,0,1:T(8,128)(2,1)}), bf16[1,24,512,256]{3,2,0,1:T(8,128)(2,1)}) %all-gather.7.cloned.1.call-update) | async-done | bytes 6291472 | tf_op jit(solution)/shard_map/all_gather | solution.py:69
  334.1 8.7 %copy.81 = bf16[1,24,512,256]{2,3,1,0:T(8,128)(2,1)} copy(bf16[1,24,512,256]{3,2,0,1:T(8,128)(2,1)} %all-gather.7.cloned.1.call-done) | data formatting | bytes 12582912 | tf_op jit(solution)/shard_map/while | solution.py:78
  342.7 173.8 %while.14 = (s32[]{:T(128)}, f32[1536,2]{0,1:T(2,128)S(1)}, f32[1536,2]{0,1:T(2,128)S(1)}, f32[1536,2,128]{0,2,1:T(8,128)S(1)}, s32[24]{0:T(128)S(1)}, /*index=5...) while((s32[]{:T(128)}, f32[1536,2]{0,1:T(2,128)S(1)}, ...), condition=%wide.region_9.10_spmd, body=%wide.region_6.9_spmd.sunk | while | flops 823400448 | bytes 23528572 | solution.py:78
  347.3 2.6 fusion.114
  361.8 2.6 fusion.114
  369.0 2.6 fusion.114
  376.3 2.6 fusion.114
  390.8 2.6 fusion.114
  398.0 2.6 fusion.114
  405.3 2.6 fusion.114
  419.7 2.6 fusion.114
  427.0 2.6 fusion.114
  434.2 2.6 fusion.114
  448.7 2.6 fusion.114
  455.9 2.6 fusion.114
  470.4 2.6 fusion.114
  477.7 2.6 fusion.114
  484.9 2.6 fusion.114
  499.4 2.6 fusion.114
  517.5 7.5 %copy.71 = bf16[1536,2,128]{2,1,0:T(2,128)(2,1)} copy(bf16[1536,2,128]{2,0,1:T(8,128)(2,1)S(1)} %divide_convert_fusion) | data formatting | bytes 1572864 | tf_op jit(solution)/shard_map/convert_element_type | solution.py:81
  525.0 7.3 %all-to-all-start.1 = ((bf16[1536,2,128]{2,1,0:T(2,128)(2,1)}), bf16[1536,2,128]{2,1,0:T(2,128)(2,1)S(1)}, u32[]{:S(2)}, u32[]{:S(2)}) async-start(bf16[1536,2,128]{2,1,0:T(2,128)(2,1)} %copy.71), calls=%async_computation.1 | async-start | bytes 1572864 | tf_op jit(solution)/shard_map/all_to_all | solution.py:82
  532.3 6.7 %copy.74 = bf16[1536,1,2,128]{3,2,0,1:T(2,128)(2,1)S(1)} copy(bf16[1536,1,2,128]{3,0,2,1:T(8,128)(2,1)} %get-tuple-element.124) | data formatting | bytes 1572864 | tf_op jit(solution)/shard_map/slice | solution.py:42
  539.5 6.5 %copy.75 = bf16[1536,1,2,128]{3,2,0,1:T(2,128)(2,1)S(1)} copy(bf16[1536,1,2,128]{3,0,2,1:T(8,128)(2,1)S(1)} %copy-done.1) | data formatting | bytes 1572864 | tf_op jit(solution)/shard_map/slice | solution.py:43
  546.6 2.8 maximum_select_fusion
  (188 shorter events, 134.6 us)
Async XLA Ops:
  7.2 3.6 copy-start.2
  7.2 194.5 %all-gather.5.cloned.1.call-start = ((), (), s32[]{:S(2)}) async-start(), calls=%async_computation.2 | async-start | bytes 7077888 | tf_op jit(solution)/shard_map/all_gather | solution.py:68
  10.0 324.0 %all-gather.7.cloned.1.call-start = ((), (), s32[]{:S(2)}) async-start(), calls=%async_computation.3 | async-start | bytes 7077888 | tf_op jit(solution)/shard_map/all_gather | solution.py:69
  13.7 44.5 %all-to-all-start = ((bf16[96,3,32,128]{3,0,1,2:T(8,128)(2,1)}), bf16[96,3,32,128]{3,0,1,2:T(8,128)(2,1)S(1)}, u32[]{:S(2)}, u32[]{:S(2)}) async-start(bf16[96,3,32,128]{3,0,1,2:T(8,128)(2,1)} %copy.58), calls=%async_computation | async-start | bytes 4718592 | tf_op jit(solution)/shard_map/all_to_all | solution.py:40
  22.1 524.5 %collective-permute-start = (bf16[2,3,512,256]{3,2,1,0:T(8,128)(2,1)}, bf16[2,3,512,256]{3,2,1,0:T(8,128)(2,1)}, u32[]{:S(2)}, u32[]{:S(2)}) collective-permute-start(bf16[2,3,512,256]{3,2,1,0:T(8,128)(2,1)} %param.6), channel_id=1, source_target_pairs={{16,0},{32,16},{48,32},{64,48},{80,64},{96,80},{112,96},{17,1},{33... | collective-permute-start | bytes 4718600 | tf_op jit(solution)/shard_map/ppermute | solution.py:13
  58.3 10.8 %copy-start = (bf16[16,96,3,2,128]{4,1,0,3,2:T(8,128)(2,1)}, bf16[16,96,3,2,128]{4,1,0,3,2:T(8,128)(2,1)S(1)}, u32[]{:S(2)}) copy-start(bf16[16,96,3,2,128]{4,1,0,3,2:T(8,128)(2,1)S(1)} %copy.60) | copy-start | bytes 7077892
  517.0 22.5 %copy-start.1 = (bf16[1536,1,2,128]{3,0,2,1:T(8,128)(2,1)S(1)}, bf16[1536,1,2,128]{3,0,2,1:T(8,128)(2,1)}, u32[]{:S(2)}) copy-start(bf16[1536,1,2,128]{3,0,2,1:T(8,128)(2,1)} %get-tuple-element.125) | copy-start | bytes 2359300
  525.0 24.4 %all-to-all-start.1 = ((bf16[1536,2,128]{2,1,0:T(2,128)(2,1)}), bf16[1536,2,128]{2,1,0:T(2,128)(2,1)S(1)}, u32[]{:S(2)}, u32[]{:S(2)}) async-start(bf16[1536,2,128]{2,1,0:T(2,128)(2,1)} %copy.71), calls=%async_computation.1 | async-start | bytes 1572864 | tf_op jit(solution)/shard_map/all_to_all | solution.py:82
Sparse Core Ops, SparseCore 0:
  10.2 191.4 all-gather.4
  203.9 130.1 all-gather.6
where the time goes:
time: 561 us; the launch traced here: 559 us
  waiting for transfers between devices  282 us (50%)
  matrix products  122 us (22%)
  local copies, waits for them, and re-layouts  66.7 us (12%)
  other arithmetic  38.3 us (7%)
  starting transfers between devices  17.1 us (3%)
  loops' own time  16.8 us (3%)
  between operations  14.9 us (3%)
    all_gather x1, waiting for transfers between devices, per_device(): key_piece = lax.all_gather(cache[0], 'section', axis=0, tiled=True)  124 us
    all_gather x1, waiting for transfers between devices, per_device(): value_piece = lax.all_gather(cache[1], 'section', axis=0, tiled=True)  124 us
    dot_general x27, matrix products, frame_update(): jnp.einsum('qhk,khd->qhd', weights.astype(jnp.bfloat16), value_block, pre...  70 us
    dot_general x27, matrix products, frame_update(): jnp.einsum('qhd,khd->qhk', query, key_block, preferred_element_type=jnp.f...  52.3 us
    all_to_all x1, waiting for transfers between devices, per_device(): lax.all_to_all(local, 'seq', split_axis=2, concat_axis=0, tiled=True)  34.1 us
    reduce_sum x26, other arithmetic, frame_update(): total = total * factor + jnp.sum(weights, axis=-1)  34 us
    another operation x1, loops' own time, per_device(): lax.scan(advance, carry, (jnp.arange(count, dtype=jnp.int32), key_rows, v...  16.8 us
    dynamic_slice x24, local copies, waits for them, and re-layouts, per_device(): lax.scan(advance, carry, (jnp.arange(count, dtype=jnp.int32), key_rows, v...  14.1 us
  transfers between devices with their start and end apart: 5, of which 3 were waited for; matrix products, arithmetic and copies ran while one was open for 40% of the time, Pallas kernels for 0%

commit v1 on v0

--- a/solution.py
+++ b/solution.py
@@ -65,7 +65,9 @@
     denoise_index = lax.axis_index("section")
     oldest = cache_frames - window[0]
     carry = state
-    key_piece = lax.all_gather(cache[0], "section", axis=0, tiled=True)
+    key_piece = jnp.concatenate(
+        lax.all_to_all(jnp.stack([cache[0]] * lax.axis_size("section")), "section", 0, 0), axis=0
+    )
     value_piece = lax.all_gather(cache[1], "section", axis=0, tiled=True)
     count = key_piece.shape[0]
     key_rows = key_piece.reshape(count, key_piece.shape[1], group, HD)

time: 561 us -> 496 us (0.88)
  waiting for transfers between devices: 282 us -> 215 us
  starting transfers between devices: 17.1 us -> 22.9 us
    all_gather x1 -> x0, waiting for transfers between devices: 124 us -> none  [per_device(): key_piece = lax.all_gather(cache[0], 'section', axis=0, tiled=True)]
    all_gather x1, waiting for transfers between devices: 124 us -> 182 us  [per_device(): value_piece = lax.all_gather(cache[1], 'section', axis=0, tiled=True)]
    all_gather x1 -> x0, local copies, waits for them, and re-layouts: 8.7 us -> none  [per_device(): key_piece = lax.all_gather(cache[0], 'section', axis=0, tiled=True)]
    all_to_all x0 -> x1, starting transfers between devices: none -> 5.8 us  [per_device(): lax.all_to_all(jnp.stack([cache[0]] * lax.axis_size('section')), 'section...]
  transfers between devices with their start and end apart: 5 -> 5, of which waited for: 3 -> 2; matrix products, arithmetic and copies ran while one was open for 40% -> 44% of each run, Pallas kernels for 0% -> 0%
where the time goes in v1:
time: 496 us; the launch traced here: 493 us
  waiting for transfers between devices  215 us (43%)
  matrix products  122 us (25%)
  local copies, waits for them, and re-layouts  64 us (13%)
  other arithmetic  38.1 us (8%)
  starting transfers between devices  22.9 us (5%)
  loops' own time  16.8 us (3%)
  between operations  14.9 us (3%)
    all_gather x1, waiting for transfers between devices, per_device(): value_piece = lax.all_gather(cache[1], 'section', axis=0, tiled=True)  182 us
    dot_general x27, matrix products, frame_update(): jnp.einsum('qhk,khd->qhd', weights.astype(jnp.bfloat16), value_block, pre...  70 us
    dot_general x27, matrix products, frame_update(): jnp.einsum('qhd,khd->qhk', query, key_block, preferred_element_type=jnp.f...  52.3 us
    reduce_sum x26, other arithmetic, frame_update(): total = total * factor + jnp.sum(weights, axis=-1)  33.9 us
    all_to_all x1, waiting for transfers between devices, per_device(): lax.all_to_all(local, 'seq', split_axis=2, concat_axis=0, tiled=True)  32.5 us
    another operation x1, loops' own time, per_device(): lax.scan(advance, carry, (jnp.arange(count, dtype=jnp.int32), key_rows, v...  16.8 us
    dynamic_slice x24, local copies, waits for them, and re-layouts, per_device(): lax.scan(advance, carry, (jnp.arange(count, dtype=jnp.int32), key_rows, v...  14.1 us
    while x3, local copies, waits for them, and re-layouts, per_device(): lax.scan(advance, carry, (jnp.arange(count, dtype=jnp.int32), key_rows, v...  11 us
  transfers between devices with their start and end apart: 5, of which 2 were waited for; matrix products, arithmetic and copies ran while one was open for 44% of the time, Pallas kernels for 0%

profile of v1, /device:TPU:1, one launch (start us, length us, event | category | flops | bytes accessed | tf_op | source)
XLA Modules:
  0.0 493.5 jit_solution(3329094356180938754)
XLA Ops:
  7.2 2.6 slice_bitcast_fusion.1
  14.4 8.4 %all-to-all-start = ((bf16[96,3,32,128]{3,0,1,2:T(8,128)(2,1)}), bf16[96,3,32,128]{3,0,1,2:T(8,128)(2,1)S(1)}, u32[]{:S(2)}, u32[]{:S(2)}) async-start(bf16[96,3,32,128]{3,0,1,2:T(8,128)(2,1)} %copy.57), calls=%async_computation | async-start | bytes 4718592 | tf_op jit(solution)/shard_map/all_to_all | solution.py:40
  26.2 32.5 %all-to-all-done = bf16[96,3,32,128]{3,0,1,2:T(8,128)(2,1)S(1)} async-done(((bf16[96,3,32,128]{3,0,1,2:T(8,128)(2,1)}), bf16[96,3,32,128]{3,0,1,2:T(8,128)(2,1)S(1)}, u32[]{:S(2)}, u32[]{:S(2)}) %all-to-all-start) | async-done | bytes 2359328 | tf_op jit(solution)/shard_map/all_to_all | solution.py:40
  58.7 3.3 stack.10
  62.0 5.8 %all-to-all-start.1 = ((bf16[8,3,512,256]{2,3,1,0:T(8,128)(2,1)}), bf16[8,3,512,256]{2,3,1,0:T(8,128)(2,1)}, u32[]{:S(2)}, u32[]{:S(2)}) async-start(bf16[8,3,512,256]{2,3,1,0:T(8,128)(2,1)} %stack.10), calls=%async_computation.1 | async-start | bytes 12582912 | tf_op jit(solution)/shard_map/all_to_all | solution.py:69
  78.6 3.8 fusion.74
  84.2 2.9 fusion.101
  87.1 182.1 %all-gather.3.cloned.1.call-done = bf16[1,24,512,256]{3,2,0,1:T(8,128)(2,1)} async-done(((bf16[1,3,512,256]{3,2,0,1:T(8,128)(2,1)}), bf16[1,24,512,256]{3,2,0,1:T(8,128)(2,1)}) %all-gather.3.cloned.1.call-update) | async-done | bytes 6291472 | tf_op jit(solution)/shard_map/all_gather | solution.py:71
  269.2 8.7 %copy.79 = bf16[1,24,512,256]{2,3,1,0:T(8,128)(2,1)} copy(bf16[1,24,512,256]{3,2,0,1:T(8,128)(2,1)} %all-gather.3.cloned.1.call-done) | data formatting | bytes 12582912 | tf_op jit(solution)/shard_map/while | solution.py:80
  277.9 173.8 %while.14 = (s32[]{:T(128)}, f32[1536,2]{0,1:T(2,128)S(1)}, f32[1536,2]{0,1:T(2,128)S(1)}, f32[1536,2,128]{0,2,1:T(8,128)S(1)}, s32[24]{0:T(128)S(1)}, /*index=5...) while((s32[]{:T(128)}, f32[1536,2]{0,1:T(2,128)S(1)}, ...), condition=%wide.region_9.10_spmd, body=%wide.region_6.9_spmd.sunk | while | flops 823400448 | bytes 23528572 | solution.py:80
  282.5 2.6 fusion.114
  289.7 2.6 fusion.114
  296.9 2.6 fusion.114
  311.4 2.6 fusion.114
  318.7 2.6 fusion.114
  333.2 2.6 fusion.114
  340.4 2.6 fusion.114
  347.6 2.6 fusion.114
  362.1 2.6 fusion.114
  369.4 2.6 fusion.114
  376.6 2.6 fusion.114
  391.1 2.6 fusion.114
  398.3 2.6 fusion.114
  405.6 2.6 fusion.114
  420.1 2.6 fusion.114
  427.3 2.6 fusion.114
  434.5 2.6 fusion.114
  452.6 7.3 %copy.69 = bf16[1536,2,128]{2,1,0:T(2,128)(2,1)} copy(bf16[1536,2,128]{2,0,1:T(8,128)(2,1)S(1)} %divide_convert_fusion) | data formatting | bytes 1572864 | tf_op jit(solution)/shard_map/convert_element_type | solution.py:83
  459.9 7.3 %all-to-all-start.2 = ((bf16[1536,2,128]{2,1,0:T(2,128)(2,1)}), bf16[1536,2,128]{2,1,0:T(2,128)(2,1)S(1)}, u32[]{:S(2)}, u32[]{:S(2)}) async-start(bf16[1536,2,128]{2,1,0:T(2,128)(2,1)} %copy.69), calls=%async_computation.2 | async-start | bytes 1572864 | tf_op jit(solution)/shard_map/all_to_all | solution.py:84
  467.2 6.7 %copy.72 = bf16[1536,1,2,128]{3,2,0,1:T(2,128)(2,1)S(1)} copy(bf16[1536,1,2,128]{3,0,2,1:T(8,128)(2,1)} %get-tuple-element.124) | data formatting | bytes 1572864 | tf_op jit(solution)/shard_map/slice | solution.py:42
  474.4 6.5 %copy.73 = bf16[1536,1,2,128]{3,2,0,1:T(2,128)(2,1)S(1)} copy(bf16[1536,1,2,128]{3,0,2,1:T(8,128)(2,1)S(1)} %copy-done.1) | data formatting | bytes 1572864 | tf_op jit(solution)/shard_map/slice | solution.py:43
  481.5 2.8 maximum_select_fusion
  (186 shorter events, 136.9 us)
Async XLA Ops:
  7.2 262.0 %all-gather.3.cloned.1.call-start = ((), (), s32[]{:S(2)}) async-start(), calls=%async_computation.3 | async-start | bytes 7077888 | tf_op jit(solution)/shard_map/all_gather | solution.py:71
  14.4 44.3 %all-to-all-start = ((bf16[96,3,32,128]{3,0,1,2:T(8,128)(2,1)}), bf16[96,3,32,128]{3,0,1,2:T(8,128)(2,1)S(1)}, u32[]{:S(2)}, u32[]{:S(2)}) async-start(bf16[96,3,32,128]{3,0,1,2:T(8,128)(2,1)} %copy.57), calls=%async_computation | async-start | bytes 4718592 | tf_op jit(solution)/shard_map/all_to_all | solution.py:40
  22.8 458.7 %collective-permute-start = (bf16[2,3,512,256]{3,2,1,0:T(8,128)(2,1)}, bf16[2,3,512,256]{3,2,1,0:T(8,128)(2,1)}, u32[]{:S(2)}, u32[]{:S(2)}) collective-permute-start(bf16[2,3,512,256]{3,2,1,0:T(8,128)(2,1)} %param.6), channel_id=1, source_target_pairs={{16,0},{32,16},{48,32},{64,48},{80,64},{96,80},{112,96},{17,1},{33... | collective-permute-start | bytes 4718600 | tf_op jit(solution)/shard_map/ppermute | solution.py:13
  62.0 215.9 %all-to-all-start.1 = ((bf16[8,3,512,256]{2,3,1,0:T(8,128)(2,1)}), bf16[8,3,512,256]{2,3,1,0:T(8,128)(2,1)}, u32[]{:S(2)}, u32[]{:S(2)}) async-start(bf16[8,3,512,256]{2,3,1,0:T(8,128)(2,1)} %stack.10), calls=%async_computation.1 | async-start | bytes 12582912 | tf_op jit(solution)/shard_map/all_to_all | solution.py:69
  68.0 10.6 %copy-start = (bf16[16,96,3,2,128]{4,1,0,3,2:T(8,128)(2,1)}, bf16[16,96,3,2,128]{4,1,0,3,2:T(8,128)(2,1)S(1)}, u32[]{:S(2)}) copy-start(bf16[16,96,3,2,128]{4,1,0,3,2:T(8,128)(2,1)S(1)} %copy.59) | copy-start | bytes 7077892
  452.1 22.3 %copy-start.1 = (bf16[1536,1,2,128]{3,0,2,1:T(8,128)(2,1)S(1)}, bf16[1536,1,2,128]{3,0,2,1:T(8,128)(2,1)}, u32[]{:S(2)}) copy-start(bf16[1536,1,2,128]{3,0,2,1:T(8,128)(2,1)} %get-tuple-element.125) | copy-start | bytes 2359300
  459.9 24.4 %all-to-all-start.2 = ((bf16[1536,2,128]{2,1,0:T(2,128)(2,1)}), bf16[1536,2,128]{2,1,0:T(2,128)(2,1)S(1)}, u32[]{:S(2)}, u32[]{:S(2)}) async-start(bf16[1536,2,128]{2,1,0:T(2,128)(2,1)} %copy.69), calls=%async_computation.2 | async-start | bytes 1572864 | tf_op jit(solution)/shard_map/all_to_all | solution.py:84
Sparse Core Ops, SparseCore 0:
  10.2 258.9 all-gather.2
